TPU v7x, 512 devices: a whole 4x4x16 slice. The times are simulated.
512 devices in a mesh: pair: 16 (over x, y), intg: 32 (over z, core).
Axes of the slice: x: 4, y: 4, z: 16, core: 2. Of those that a mesh axis runs over, the one named last changes fastest.
Arguments:
- amplitudes: bfloat16 [2048, 12288], P('pair', 'intg'), may hold values from -6 to 6
- integrals: bfloat16 [32, 32, 5, 128, 128], P('intg', None, None, 'pair'), may hold values from -0.0390625 to 0.0390625
- cd_index: int32 [32, 32, 5], replicated, may hold values from 0 to 2
- ab_index: int32 [32, 32, 5], replicated, may hold values from 0 to 31
- owner_map: int32 [32], replicated, may hold values from 0 to 31, each once
Outputs:
- residual: bfloat16 [2048, 4096], P('pair', 'intg')
Inputs may be any that keep to these rules, and one draw needn't show every extreme that they name: owner_map is a permutation of the residual tile columns.
All inputs are finite; a program needn't handle non-finite values.
Results may differ from a plain program's by a relative error of at most 0.00175.
Values may be sent and summed in bfloat16 or wider, within the bound.
A program may use at most 64 MiB of HBM per device.

v0:
```python
import math

import jax
import jax.numpy as jnp
from jax import lax
from jax.sharding import PartitionSpec as P


def slot_of(owner_map, targets):
    count = owner_map.shape[0]
    match = owner_map[None, :] == targets.reshape(-1)[:, None]
    places = jnp.arange(count, dtype=jnp.int32)[None, :]
    return jnp.sum(jnp.where(match, places, 0), axis=1)


def ladder(columns, tiles, cd_global, slot_index, res_count):
    row_count = columns.shape[0]
    tile_size = tiles.shape[-1]
    blocks = columns.reshape(row_count, -1, tile_size)
    total_tiles = tiles.shape[0]
    group = math.gcd(total_tiles, 8)
    tiles_grouped = tiles.reshape(total_tiles // group, group, tile_size, tile_size)
    cd_grouped = cd_global.reshape(-1, group)
    slot_grouped = slot_index.reshape(-1, group)

    def accumulate(partial_value, entries):
        tile_block, cd_block, slot_block = entries
        picked = jnp.take(blocks, cd_block, axis=1)
        products = jnp.einsum(
            "rgc,gcd->grd", picked, tile_block, preferred_element_type=jnp.float32
        )
        return (partial_value.at[slot_block].add(products), None)

    partial_value = jnp.zeros((res_count, row_count, tile_size), jnp.float32)
    partial_value, unused = lax.scan(
        accumulate, partial_value, (tiles_grouped, cd_grouped, slot_grouped)
    )
    return partial_value


def per_device(amplitudes, integrals, cd_index, ab_index, owner_map):
    group_size = lax.axis_size("intg")
    position = lax.axis_index("intg")
    full_rows = lax.all_gather(integrals, "pair", axis=3, tiled=True)
    tile_size = full_rows.shape[-1]
    kt_local = amplitudes.shape[1] // tile_size
    columns = lax.all_gather(amplitudes, "intg", axis=1, tiled=True)
    local_cd = lax.dynamic_index_in_dim(cd_index, position, 0, keepdims=False)
    holders = jnp.arange(group_size, dtype=jnp.int32)[:, None]
    cd_global = (holders * kt_local + local_cd).reshape(-1)
    targets = lax.dynamic_index_in_dim(ab_index, position, 0, keepdims=False)
    tiles = full_rows.reshape(-1, tile_size, tile_size)
    slot_index = slot_of(owner_map, targets)
    partial_value = ladder(columns, tiles, cd_global, slot_index, owner_map.shape[0])
    summed = lax.psum_scatter(partial_value, "intg", scatter_dimension=0, tiled=True)
    return summed.reshape(summed.shape[1], tile_size).astype(jnp.bfloat16)


def solution(mesh):
    return jax.shard_map(
        per_device,
        mesh=mesh,
        in_specs=(P("pair", "intg"), P("intg", None, None, "pair", None), P(), P(), P()),
        out_specs=P("pair", "intg"),
        check_vma=False,
    )
```

profile of v0, /device:TPU:6, one launch (start us, length us, event | category | flops | bytes accessed | tf_op | source)
XLA Modules:
  0.0 381.2 jit_solution(9271142029711433298)
XLA Ops:
  6.5 1.6 copy.16
  11.1 75.8 %all-gather.3.cloned.1.call-done = bf16[128,12288]{0,1:T(8,128)(2,1)} async-done(((bf16[128,384]{0,1:T(8,128)(2,1)}), bf16[128,12288]{0,1:T(8,128)(2,1)}) %all-gather.3.cloned.1.call-update) | async-done | bytes 3145744 | tf_op jit(solution)/shard_map/all_gather | solution.py:47
  87.0 4.7 %copy.17 = bf16[128,96,128]{2,0,1:T(8,128)(2,1)} copy(bf16[128,96,128]{0,2,1:T(8,128)(2,1)} %bitcast.34) | data formatting | bytes 6291456 | tf_op jit(solution)/shard_map/while | solution.py:35
  91.7 73.1 %all-gather.5.cloned.1.call-done = bf16[1,32,5,128,128]{4,3,2,1,0:T(8,128)(2,1)} async-done(((bf16[1,32,5,8,128]{4,3,2,1,0:T(8,128)(2,1)}), bf16[1,32,5,128,128]{4,3,2,1,0:T(8,128)(2,1)}) %all-gather.5.cloned.1.call-update) | async-done | bytes 5242896 | tf_op jit(solution)/shard_map/all_gather | solution.py:44
  165.0 96.9 %while.10 = (s32[]{:T(128)}, f32[32,128,128]{2,1,0:T(8,128)S(1)}, s32[20,8]{1,0:T(8,128)S(1)}, s32[20,8]{1,0:T(8,128)S(1)}, bf16[128,96,128]{2,0,1:T(8,128)(2,1)}, /*index=5*/bf16[20,8,128,128]{3,2,1,0:T(8,128)(2,1)}, s32[]{:T(128)}) while((s32[]{:T(128)}, f32[32,128,128]{2,1,0:T(8,128)S(1)}, s32[20,8]{1,0:T(8,128)S(1)}, ...), condition=%wide.region_3.4_spmd, body=%wide.region_1.3_spmd.sunk | while | flops 33817696 | bytes 3150193 | solution.py:35
  165.0 2.5 gather_fusion
  167.5 1.2 fusion.19
  168.8 1.0 scatter_fusion
  169.9 2.5 gather_fusion
  172.4 1.2 fusion.19
  174.7 2.5 gather_fusion
  177.2 1.2 fusion.19
  179.6 2.5 gather_fusion
  182.1 1.2 fusion.19
  183.3 1.0 scatter_fusion
  184.4 2.5 gather_fusion
  186.9 1.2 fusion.19
  188.1 1.0 scatter_fusion
  189.3 2.5 gather_fusion
  191.8 1.2 fusion.19
  193.0 1.0 scatter_fusion
  194.1 2.5 gather_fusion
  196.6 1.2 fusion.19
  198.9 2.5 gather_fusion
  201.4 1.2 fusion.19
  202.7 1.0 scatter_fusion
  203.8 2.5 gather_fusion
  206.3 1.2 fusion.19
  207.5 1.0 scatter_fusion
  208.6 2.5 gather_fusion
  211.1 1.2 fusion.19
  212.4 1.0 scatter_fusion
  213.5 2.5 gather_fusion
  216.0 1.2 fusion.19
  217.2 1.0 scatter_fusion
  218.3 2.5 gather_fusion
  220.8 1.2 fusion.19
  222.0 1.0 scatter_fusion
  223.2 2.5 gather_fusion
  225.7 1.2 fusion.19
  226.9 1.0 scatter_fusion
  228.0 2.5 gather_fusion
  230.5 1.2 fusion.19
  231.7 1.0 scatter_fusion
  232.9 2.5 gather_fusion
  235.3 1.2 fusion.19
  236.6 1.0 scatter_fusion
  237.7 2.5 gather_fusion
  240.2 1.2 fusion.19
  241.4 1.0 scatter_fusion
  242.5 2.5 gather_fusion
  245.0 1.2 fusion.19
  246.3 1.0 scatter_fusion
  247.4 2.5 gather_fusion
  249.9 1.2 fusion.19
  252.2 2.5 gather_fusion
  254.7 1.2 fusion.19
  256.0 1.0 scatter_fusion
  257.1 2.5 gather_fusion
  259.6 1.2 fusion.19
  260.8 1.0 scatter_fusion
  261.9 1.3 copy-done
  263.2 110.0 %reduce-scatter.2.cloned.1.call-done = f32[1,128,128]{2,1,0:T(8,128)} async-done(((f32[32,128,128]{2,1,0:T(8,128)}), f32[1,128,128]{2,1,0:T(8,128)}) %reduce-scatter.2.cloned.1.call-update) | async-done | bytes 65552 | tf_op jit(solution)/shard_map/reduce_scatter | solution.py:55
  373.2 1.5 convert_bitcast_fusion
  (83 shorter events, 8.0 us)
Async XLA Ops:
  6.5 80.4 %all-gather.3.cloned.1.call-start = ((), (), s32[]{:S(2)}) async-start(), calls=%async_computation.1 | async-start | bytes 3244032 | tf_op jit(solution)/shard_map/all_gather | solution.py:47
  8.2 156.6 %all-gather.5.cloned.1.call-start = ((), (), s32[]{:S(2)}) async-start(), calls=%async_computation.2 | async-start | bytes 5570560 | tf_op jit(solution)/shard_map/all_gather | solution.py:44
  8.9 364.2 %reduce-scatter.2.cloned.1.call-start = ((), (), s32[]{:S(2)}) async-start(), calls=%async_computation.3 | async-start | bytes 2162688 | tf_op jit(solution)/shard_map/reduce_scatter | solution.py:55
  261.9 1.3 copy-start
Sparse Core Ops, SparseCore 0:
  9.5 77.4 all-gather.2
  90.0 74.7 all-gather.4
  263.3 109.8 reduce-scatter.1
where the time goes:
time: 383 us; the launch traced here: 381 us
  waiting for transfers between devices  260 us (68%)
  local copies, waits for them, and re-layouts  59 us (15%)
  matrix products  24.7 us (6%)
  other arithmetic  23.6 us (6%)
  between operations  13.2 us (3%)
    reduce_scatter x1, waiting for transfers between devices, per_device(): lax.psum_scatter(partial_value, 'intg', scatter_dimension=0, tiled=True)  110 us
    all_gather x1, waiting for transfers between devices, per_device(): columns = lax.all_gather(amplitudes, 'intg', axis=1, tiled=True)  75.8 us
    all_gather x1, waiting for transfers between devices, per_device(): full_rows = lax.all_gather(integrals, 'pair', axis=3, tiled=True)  73.1 us
    gather x20, local copies, waits for them, and re-layouts, accumulate(): picked = jnp.take(blocks, cd_block, axis=1)  49.7 us
    dot_general x20, matrix products, accumulate(): jnp.einsum('rgc,gcd->grd', picked, tile_block, preferred_element_type=jnp...  24.7 us
    scatter-add x20, other arithmetic, accumulate(): return (partial_value.at[slot_block].add(products), None)  20.7 us
  transfers between devices with their start and end apart: 3, of which 3 were waited for; matrix products, arithmetic and copies ran while one was open for 2% of the time, Pallas kernels for 0%

commit v1 on v0

v1 whole, which is shorter than its diff:
```python
import jax
import jax.numpy as jnp
from jax import lax
from jax.experimental import pallas as pl
from jax.experimental.pallas import tpu as pltpu
from jax.sharding import PartitionSpec as P

MESH = pl.DeviceIdType.MESH
NX, NY, NZ = 4, 4, 16
CORES = 2
T = 128
KT = 3
CAP = 5
NI = NZ * CORES
TILES = NI * CAP
ROWS = 8
SHARD = TILES * ROWS
HALF = SHARD // 2
QUARTER = HALF // 2
NP = NX * NY
RES = 32
FAR = NZ // 2
UNROLL = 2


def index_table(cd_index, ab_index, owner_map):
    position = lax.axis_index("intg")
    cd = lax.dynamic_index_in_dim(cd_index, position, 0, keepdims=False).reshape(-1)
    ab = lax.dynamic_index_in_dim(ab_index, position, 0, keepdims=False).reshape(-1)
    order = jnp.arange(TILES, dtype=jnp.int32)
    holder = order // CAP
    amp = (holder % CORES) * (NZ * KT) + (holder // CORES) * KT + cd
    slots = jnp.arange(RES, dtype=jnp.int32)
    slot = jnp.sum(jnp.where(owner_map[None, :] == ab[:, None], slots[None, :], 0), axis=1)
    key = slot * TILES + order
    rank = jnp.sum((key[None, :] < key[:, None]).astype(jnp.int32), axis=1)
    hit = rank[None, :] == order[:, None]
    perm = jnp.sum(jnp.where(hit, order[None, :], 0), axis=1)
    sorted_slot = jnp.sum(jnp.where(hit, slot[None, :], 0), axis=1)
    before = jnp.concatenate([jnp.full((1,), -1, jnp.int32), sorted_slot[:-1]])
    keep = (sorted_slot == before).astype(jnp.int32)
    upto = jnp.sum((slot[None, :] <= slots[:, None]).astype(jnp.int32), axis=1)
    used = jnp.any(slot[None, :] == slots[:, None], axis=1).astype(jnp.int32)
    last = jnp.maximum(upto - 1, 0)
    return jnp.concatenate([amp, perm, keep, last, used])


AMP, PERM, KEEP, LAST, USED = 0, TILES, 2 * TILES, 3 * TILES, 3 * TILES + RES


def kernel(
    table, amp_hbm, int_hbm, out_ref,
    gath, amps, prods, sums, own, cross, ring_in, ring_out,
    local_sem, xy_send, xy_recv, z_send, z_recv, c_send, c_recv,
    x_send, x_recv, r_send, r_recv,
):
    p = lax.axis_index("pair")
    g = lax.axis_index("intg")
    x, y = p // NY, p % NY
    z, core = g // CORES, g % CORES
    sib = 1 - core

    def at_x(d):
        return ((x + d + NX) % NX, y)

    def at_y(d):
        return (x, (y + d + NY) % NY)

    def z_at(d):
        return (z + d + 2 * NZ) % NZ

    def flat(xy):
        return xy[0] * NY + xy[1]

    def xy_dev(xy):
        return (flat(xy), g)

    def z_dev(d):
        return (p, z_at(d) * CORES + core)

    sib_dev = (p, z * CORES + sib)

    def remote(src, dst, ss, rs, to):
        return pltpu.make_async_remote_copy(
            src_ref=src, dst_ref=dst, send_sem=ss, recv_sem=rs, device_id=to, device_id_type=MESH
        )

    barrier = pltpu.get_barrier_semaphore()
    partners = [xy_dev(at_x(1)), xy_dev(at_x(-1)), xy_dev(at_y(1)), xy_dev(at_y(-1)), z_dev(1), z_dev(-1), sib_dev]
    for to in partners:
        pl.semaphore_signal(barrier, inc=1, device_id=to, device_id_type=MESH)

    own_copy = pltpu.make_async_copy(int_hbm, gath.at[p], local_sem.at[0])
    own_copy.start()
    amp_copies = []
    for q in range(KT):
        c = pltpu.make_async_copy(
            amp_hbm.at[:, pl.ds(q * T, T)], amps.at[core, z * KT + q], local_sem.at[1 + q]
        )
        c.start()
        amp_copies.append(c)
    pl.semaphore_wait(barrier, len(partners))

    xy_sends = []

    def place(h, da, db):
        ax, by = (da, db) if h == 0 else (db, da)
        return ((x + ax + NX) % NX, (y + by + NY) % NY)

    def rows_of(h, part):
        if part is None:
            return h * HALF, HALF
        return h * HALF + part * QUARTER, QUARTER

    def xy_copy(h, sem, who, to, part, own=False):
        start, count = rows_of(h, part)
        src = int_hbm if own else gath.at[flat(who)]
        return remote(
            src.at[pl.ds(start, count)], gath.at[flat(who), pl.ds(start, count)],
            xy_send.at[h, sem], xy_recv.at[h, sem], xy_dev(to),
        )

    def xy_start(h, sem, who, to, part, own=False):
        c = xy_copy(h, sem, who, to, part, own)
        c.start()
        xy_sends.append(c)

    def xy_wait(h, sem, who, part):
        xy_copy(h, sem, who, place(h, 0, 1), part).wait_recv()

    SHIFT = (0, -1, 1, 2)

    def first_own(h):
        me = place(h, 0, 0)
        xy_start(h, 0, me, place(h, 1, 0), None, True)
        xy_start(h, 1, me, place(h, -1, 0), None, True)

    def second(h, q, own=False):
        who = place(h, SHIFT[q], 0)
        xy_start(h, 4 + 4 * q, who, place(h, 0, 1), None, own)
        xy_start(h, 5 + 4 * q, who, place(h, 0, -1), None, own)

    def first_forward(h, side):
        who = place(h, -1 if side == 0 else 1, 0)
        xy_wait(h, side, who, None)
        xy_start(h, 2 + side, who, place(h, 1 if side == 0 else -1, 0), side)

    def first_far(h):
        who = place(h, 2, 0)
        xy_wait(h, 2, who, 0)
        xy_wait(h, 3, who, 1)

    def second_forward(h, q):
        for side in (0, 1):
            who = place(h, SHIFT[q], -1 if side == 0 else 1)
            xy_wait(h, 4 + 4 * q + side, who, None)
            xy_start(h, 6 + 4 * q + side, who, place(h, 0, 1 if side == 0 else -1), side)

    def second_far(h, q):
        who = place(h, SHIFT[q], 2)
        xy_wait(h, 6 + 4 * q, who, 0)
        xy_wait(h, 7 + 4 * q, who, 1)

    z_sends = []

    def shard(d):
        return amps.at[core, pl.ds(z_at(d) * KT, KT)]

    def z_start(way, step):
        d = -step if way == 0 else step
        c = remote(shard(d), shard(d), z_send.at[way, step], z_recv.at[way, step], z_dev(1 if way == 0 else -1))
        c.start()
        z_sends.append(c)

    def z_wait(way, step):
        d = -step - 1 if way == 0 else step + 1
        remote(shard(d), shard(d), z_send.at[way, step], z_recv.at[way, step], z_dev(1)).wait_recv()

    def to_sibling(d):
        remote(shard(d), shard(d), c_send, c_recv, sib_dev).start()

    def z_step(step):
        for way in (0, 1):
            steps = FAR if way == 0 else FAR - 1
            if step >= steps:
                continue
            z_wait(way, step)
            if step + 1 < steps:
                z_start(way, step + 1)
            to_sibling(-step - 1 if way == 0 else step + 1)

    for h in (0, 1):
        first_own(h)
    for c in amp_copies:
        c.wait()
    z_start(0, 0)
    z_start(1, 0)
    for h in (0, 1):
        second(h, 0, True)
    to_sibling(0)
    z_step(0)
    for h in (0, 1):
        for side in (0, 1):
            first_forward(h, side)
            second(h, 1 + side)
    z_step(1)
    z_step(2)
    for h in (0, 1):
        second_forward(h, 0)
    for h in (0, 1):
        first_far(h)
        second(h, 3)
    z_step(3)
    z_step(4)
    for h in (0, 1):
        second_forward(h, 1)
    z_step(5)
    for h in (0, 1):
        second_forward(h, 2)
    z_step(6)
    z_step(7)
    for h in (0, 1):
        second_forward(h, 3)
    own_copy.wait()
    remote(amps.at[core], amps.at[sib], c_send, c_recv, sib_dev).wait()
    for h in (0, 1):
        for q in range(4):
            second_far(h, q)
    for c in xy_sends + z_sends:
        c.wait_send()

    def products(step, carry):
        for k in range(UNROLL):
            u = step * UNROLL + k
            group = gath[:, pl.ds(pl.multiple_of(u * 2 * ROWS, 2 * ROWS), 2 * ROWS), :].astype(jnp.float32)
            for odd in (0, 1):
                tile = group[:, odd * ROWS : (odd + 1) * ROWS, :].reshape(T, T).astype(jnp.bfloat16)
                a = table[AMP + 2 * u + odd]
                prods[2 * u + odd] = jnp.dot(amps[a // (NZ * KT), a % (NZ * KT)], tile, preferred_element_type=jnp.float32)
        return carry

    lax.fori_loop(0, TILES // 2 // UNROLL, products, 0)

    def running(t, acc):
        acc = jnp.where(table[KEEP + t] > 0, acc, 0.0) + prods[table[PERM + t]]
        sums[t] = acc
        return acc

    lax.fori_loop(0, TILES, running, jnp.zeros((T, T), jnp.float32))

    def pick(r, carry):
        own[r] = jnp.where(table[USED + r] > 0, sums[table[LAST + r]], 0.0)
        return carry

    lax.fori_loop(0, RES, pick, 0)

    far_first = [FAR]
    for d in range(FAR - 1, 0, -1):
        far_first += [d, -d]
    far_first.append(0)
    x_sends = {}
    for n, d in enumerate(far_first):
        c = remote(own.at[z_at(d) * CORES + sib], cross.at[n], x_send.at[n], x_recv.at[n], sib_dev)
        c.start()
        x_sends[d] = c

    hrows = T // 2
    r_sends = []

    def ring(way, step, part):
        rows = pl.ds(part * hrows, hrows)
        return remote(
            ring_out.at[way, step, rows], ring_in.at[way, step, rows],
            r_send.at[way, step, part], r_recv.at[way, step, part], z_dev(1 if way == 0 else -1),
        )

    def total(d, part):
        rows = pl.ds(part * hrows, hrows)
        return own[z_at(d) * CORES + core, rows, :] + cross[far_first.index(d), rows, :]

    x_sends[FAR].wait()
    for way in (0, 1):
        ring_out[way, 0, way * hrows : (way + 1) * hrows, :] = total(FAR, way)
        c = ring(way, 0, way)
        c.start()
        r_sends.append(c)
    for step in range(1, FAR):
        for way in (0, 1):
            d = FAR - step if way == 0 else step - FAR
            x_sends[d].wait()
            for part in ((way, 1 - way) if step == 1 else (0, 1)):
                value = total(d, part)
                if step > 1 or part == way:
                    ring(way, step - 1, part).wait_recv()
                    value = value + ring_in[way, step - 1, part * hrows : (part + 1) * hrows, :]
                ring_out[way, step, part * hrows : (part + 1) * hrows, :] = value
                c = ring(way, step, part)
                c.start()
                r_sends.append(c)
    x_sends[0].wait()
    for part in (0, 1):
        value = total(0, part)
        for way in (0, 1):
            ring(way, FAR - 1, part).wait_recv()
            value = value + ring_in[way, FAR - 1, part * hrows : (part + 1) * hrows, :]
        out_ref[part * hrows : (part + 1) * hrows, :] = value.astype(jnp.bfloat16)
    for c in r_sends:
        c.wait_send()


def per_device(amplitudes, integrals, cd_index, ab_index, owner_map):
    table = index_table(cd_index, ab_index, owner_map)
    shard = integrals.reshape(SHARD, T)
    dma = pltpu.SemaphoreType.DMA
    return pl.pallas_call(
        kernel,
        out_shape=jax.ShapeDtypeStruct((T, T), jnp.bfloat16),
        in_specs=[
            pl.BlockSpec(memory_space=pltpu.SMEM),
            pl.BlockSpec(memory_space=pl.ANY),
            pl.BlockSpec(memory_space=pl.ANY),
        ],
        out_specs=pl.BlockSpec(memory_space=pltpu.VMEM),
        scratch_shapes=[
            pltpu.VMEM((NP, SHARD, T), jnp.bfloat16),
            pltpu.VMEM((CORES, NZ * KT, T, T), jnp.bfloat16),
            pltpu.VMEM((TILES, T, T), jnp.float32),
            pltpu.VMEM((TILES, T, T), jnp.float32),
            pltpu.VMEM((RES, T, T), jnp.float32),
            pltpu.VMEM((NZ, T, T), jnp.float32),
            pltpu.VMEM((2, FAR, T, T), jnp.float32),
            pltpu.VMEM((2, FAR, T, T), jnp.float32),
            dma((1 + KT,)),
            dma((2, 20)), dma((2, 20)),
            dma((2, FAR)), dma((2, FAR)),
            dma, dma,
            dma((NZ,)), dma((NZ,)),
            dma((2, FAR, 2)), dma((2, FAR, 2)),
        ],
        compiler_params=pltpu.CompilerParams(
            collective_id=0, has_side_effects=True, vmem_limit_bytes=52 * 1024 * 1024
        ),
        name="ladder",
    )(table, amplitudes, shard)


def solution(mesh):
    return jax.shard_map(
        per_device,
        mesh=mesh,
        in_specs=(P("pair", "intg"), P("intg", None, None, "pair", None), P(), P(), P()),
        out_specs=P("pair", "intg"),
        check_vma=False,
    )
```

time: 383 us -> 96.3 us (0.25)
  waiting for transfers between devices: 260 us -> 0 us
  Pallas kernels: 0 us -> 91.1 us
  local copies, waits for them, and re-layouts: 59 us -> 2.84 us
  matrix products: 24.7 us -> 0 us
  other arithmetic: 23.6 us -> 1.45 us
  between operations: 13.2 us -> 0.05 us
    all_gather x2 -> x0, waiting for transfers between devices: 149 us -> none  [the longest x1 75.8 us: per_device(): columns = lax.all_gather(amplitudes, 'intg', axis=1, tiled=True)]
    reduce_scatter x1 -> x0, waiting for transfers between devices: 110 us -> none  [per_device(): lax.psum_scatter(partial_value, 'intg', scatter_dimension=0, tiled=True)]
    pallas_call x0 -> x1, Pallas kernels: none -> 91.1 us  [per_device(): pl.pallas_call(kernel, out_shape=jax.ShapeDtypeStruct((T, T), jnp.bfloat1...]
    gather x20 -> x0, local copies, waits for them, and re-layouts: 49.7 us -> none  [accumulate(): picked = jnp.take(blocks, cd_block, axis=1)]
    dot_general x20 -> x0, matrix products: 24.7 us -> none  [accumulate(): jnp.einsum('rgc,gcd->grd', picked, tile_block, preferred_element_type=jnp...]
    scatter-add x20 -> x0, other arithmetic: 20.7 us -> none  [accumulate(): return (partial_value.at[slot_block].add(products), None)]
    while x1 -> x0, local copies, waits for them, and re-layouts: 4.71 us -> none  [ladder(): lax.scan(accumulate, partial_value, (tiles_grouped, cd_grouped, slot_grou...]
  transfers between devices with their start and end apart: 3 -> 0, of which waited for: 3 -> 0; matrix products, arithmetic and copies ran while one was open for 2% -> 0% of each run, Pallas kernels for 0% -> 0%
where the time goes in v1:
time: 96.3 us; the launch traced here: 95.4 us
  Pallas kernels  91.1 us (95%)
  local copies, waits for them, and re-layouts  2.84 us (3%)
  other arithmetic  1.45 us (2%)
    pallas_call x1, Pallas kernels, per_device(): pl.pallas_call(kernel, out_shape=jax.ShapeDtypeStruct((T, T), jnp.bfloat1...  91.1 us

profile of v1, /device:TPU:6, one launch (start us, length us, event | category | flops | bytes accessed | tf_op | source)
XLA Modules:
  0.0 95.4 jit_solution(18107945667177341694)
XLA Ops:
  0.0 0.0 copy-start.1
  0.0 0.8 constant_dynamic-slice_fusion
  0.8 0.1 copy.9
  0.9 0.1 eq.21
  1.0 0.7 select_reduce_fusion.2
  1.7 0.1 fusion
  1.9 0.1 convert_reduce_fusion.1
  2.0 0.2 convert_reduce_fusion
  2.2 0.2 select_reduce_fusion
  2.4 0.1 compare_convert_fusion
  2.4 0.1 copy.8
  2.5 0.1 reshape.26
  2.7 0.1 concatenate.7.table
  2.7 0.0 copy-done.1
  2.7 0.0 copy-start
  2.7 1.0 %copy-done = bf16[1,32,5,8,128]{4,3,2,1,0:T(8,128)(2,1)S(1)} copy-done((bf16[1,32,5,8,128]{4,3,2,1,0:T(8,128)(2,1)S(1)}, bf16[1,32,5,8,128]{4,3,2,1,0:T(8,128)(2,1)}, u32[]{:S(2)}) %copy-start) | copy-done | bytes 327704
  3.7 91.1 %ladder.1 = bf16[128,128]{1,0:T(8,128)(2,1)S(1)} custom-call(s32[544]{0:T(1024)S(1)} %concatenate.7.table, bf16[128,384]{1,0:T(8,128)(2,1)S(1)} %copy-done.1, bf16[1280,128]{1,0:T(8,128)(2,1)S(1)} %bitcast.2), custom_call_target="tpu_custom_call" | custom-call | tf_op jit(solution)/shard_map/ladder/pallas_call | solution.py:315
  94.8 0.6 copy.11
  (4 shorter events, 0.0 us)
Async XLA Ops:
  0.0 2.7 %copy-start.1 = (bf16[128,384]{1,0:T(8,128)(2,1)S(1)}, bf16[128,384]{1,0:T(8,128)(2,1)}, u32[]{:S(2)}) copy-start(bf16[128,384]{1,0:T(8,128)(2,1)} %amp_hbm.1) | copy-start | bytes 294916
  2.7 1.0 %copy-start = (bf16[1,32,5,8,128]{4,3,2,1,0:T(8,128)(2,1)S(1)}, bf16[1,32,5,8,128]{4,3,2,1,0:T(8,128)(2,1)}, u32[]{:S(2)}) copy-start(bf16[1,32,5,8,128]{4,3,2,1,0:T(8,128)(2,1)} %param.6) | copy-start | bytes 983044

commit v2 on v0

v2 whole, which is shorter than its diff:
```python
import jax
import jax.numpy as jnp
from jax import lax
from jax.experimental import pallas as pl
from jax.experimental.pallas import tpu as pltpu
from jax.sharding import PartitionSpec as P

MESH = pl.DeviceIdType.MESH
NX, NY, NZ = 4, 4, 16
CORES = 2
T = 128
KT = 3
CAP = 5
NI = NZ * CORES
TILES = NI * CAP
ROWS = 8
SHARD = TILES * ROWS
NP = NX * NY
RES = 32
FAR = NZ // 2
BATCHES = 2
BATCH_TILES = TILES // BATCHES
CHUNK = SHARD // BATCHES // 2
QUAD_TILES = BATCH_TILES // 2
PIECE = CHUNK // 2
QUAD = 4
SOON = 5
JUMP_SUM = 5
PARTS = 4
UNROLL = 2
VMEM = 60 * 1024 * 1024


def quad_of(z, batch, half):
    side = 2 * ((z % QUAD) // 2) - 1
    step = (0, side, -side, 2)[2 * batch + half]
    return (z // QUAD + step + QUAD) % QUAD


PERM, KEEP, LAST, USED, WHICH = 0, 1, 2, 3, 4
GROUPS = BATCHES * RES
WIDE = 256


def iota(shape, dim):
    return lax.broadcasted_iota(jnp.int32, shape, dim)


def inside(value, count):
    return jnp.minimum(jnp.maximum(value, 0), count - 1)


def place_table(table, cd, ab, owner, z, g):
    f32, bf16 = jnp.float32, jnp.bfloat16

    def dot(a, b, dims=((1,), (0,))):
        return lax.dot_general(a.astype(bf16), b.astype(bf16), (dims, ((), ())), preferred_element_type=f32)

    eye = iota((RES, RES), 0) == iota((RES, RES), 1)
    owners = jnp.sum(jnp.where(eye, owner[...].astype(f32), 0.0), axis=1, keepdims=True)
    quad = iota((1, NI), 1) // (QUAD * CORES)
    early = (quad == quad_of(z, 0, 0)) | (quad == quad_of(z, 0, 1))
    member = jnp.zeros((GROUPS, WIDE), f32)
    for s in range(CAP):
        hit = owners == ab[s, pl.ds(g, 1), :].astype(f32)
        both = jnp.concatenate([jnp.where(hit & early, 1.0, 0.0), jnp.where(hit & ~early, 1.0, 0.0)], axis=0)
        spread = jnp.where(iota((NI, WIDE), 1) == iota((NI, WIDE), 0) + s * NI, 1.0, 0.0)
        member = member + dot(both, spread)
    before = dot(member, jnp.where(iota((WIDE, WIDE), 0) < iota((WIDE, WIDE), 1), 1.0, 0.0))
    counts = jnp.sum(member, axis=1, keepdims=True)
    lower = jnp.where(iota((GROUPS, GROUPS), 1) < iota((GROUPS, GROUPS), 0), 1.0, 0.0)
    starts = dot(lower, jnp.broadcast_to(counts, (GROUPS, T)))[:, :1]
    rank = jnp.sum(member * (starts + before), axis=0, keepdims=True).astype(jnp.int32)
    lane = iota((WIDE, WIDE), 1)
    moved = jnp.where((iota((WIDE, WIDE), 0) == rank) & (lane < TILES), 1.0, 0.0)
    tile = iota((8, WIDE), 1) % NI * CAP + iota((8, WIDE), 1) // NI
    perm = dot(tile, moved, ((1,), (1,)))
    full = counts > 0.0
    first = (iota((GROUPS, WIDE), 1).astype(f32) == starts) & full
    same = iota((GROUPS, WIDE), 1) == iota((GROUPS, WIDE), 0)
    last = jnp.where(same, jnp.clip(starts + counts - 1.0, 0.0, TILES - 1.0), 0.0)
    top = TILES - 1.0
    table[PERM : PERM + 1, :] = jnp.minimum(perm[:1], top).astype(jnp.int32)
    table[KEEP : KEEP + 1, :] = 1 - jnp.max(jnp.where(first, 1.0, 0.0), axis=0, keepdims=True).astype(jnp.int32)
    table[LAST : LAST + 1, :] = jnp.sum(last, axis=0, keepdims=True).astype(jnp.int32)
    table[USED : USED + 1, :] = jnp.max(jnp.where(same & full, 1.0, 0.0), axis=0, keepdims=True).astype(jnp.int32)
    for s in range(CAP):
        table[WHICH + s : WHICH + s + 1, :NI] = cd[s, pl.ds(g, 1), :]


def kernel(
    cd_hbm, ab_hbm, owner, amp_hbm, int_hbm, out_ref,
    table, cd, ab, table_vmem, index_sem,
    gath, amps, stage, prods, sums, own, cross, ring_in, ring_out,
    own_sem, amp_sem, xy_send, xy_recv, z_send, z_recv, c_send, c_recv,
    x_send, x_recv, r_send, r_recv,
):
    p = lax.axis_index("pair")
    g = lax.axis_index("intg")
    x, y = p // NY, p % NY
    z, core = g // CORES, g % CORES
    sib = 1 - core

    def flat(xy):
        return xy[0] * NY + xy[1]

    def xy_dev(xy):
        return (flat(xy), g)

    def z_at(d):
        return (z + d + 2 * NZ) % NZ

    def z_dev(d):
        return (p, z_at(d) * CORES + core)

    sib_dev = (p, z * CORES + sib)

    def remote(src, dst, ss, rs, to):
        return pltpu.make_async_remote_copy(
            src_ref=src, dst_ref=dst, send_sem=ss, recv_sem=rs, device_id=to, device_id_type=MESH
        )

    def place(h, da, db):
        ax, by = (da, db) if h == 0 else (db, da)
        return ((x + ax + NX) % NX, (y + by + NY) % NY)

    barrier = pltpu.get_barrier_semaphore()
    partners = [xy_dev(place(h, d, 0)) for h in (0, 1) for d in (1, -1)] + [sib_dev]
    partners += [z_dev(1), z_dev(-1)]
    for to in partners:
        pl.semaphore_signal(barrier, inc=1, device_id=to, device_id_type=MESH)

    own_copy = pltpu.make_async_copy(int_hbm, gath.at[p], own_sem)
    own_copy.start()
    own_amps = amps.at[pl.ds(core * (NZ * KT) + z * KT, KT)]
    for q in range(KT):
        pltpu.make_async_copy(amp_hbm.at[:, pl.ds(q * T, T)], own_amps.at[q], amp_sem).start()
    index_copies = [
        pltpu.make_async_copy(cd_hbm, cd, index_sem.at[0]), pltpu.make_async_copy(ab_hbm, ab, index_sem.at[1])
    ]
    for c in index_copies:
        c.start()
    pl.semaphore_wait(barrier, len(partners))

    SHIFT = (0, -1, 1, 2)
    FIRST, FIRST_FAR, SECOND, SECOND_FAR = 0, 1, 2, 6

    def xy_start(b, h, sem, who, to, part=None, own=False):
        start, count = pl.multiple_of(quad_of(z, b, h) * CHUNK, CHUNK), CHUNK
        if part is not None:
            start, count = start + part * PIECE, PIECE
        src = int_hbm if own else gath.at[flat(who)]
        remote(
            src.at[pl.ds(start, count)], gath.at[flat(who), pl.ds(start, count)],
            xy_send, xy_recv.at[b, sem], xy_dev(to),
        ).start()

    def xy_wait(b, sem, chunks):
        if chunks * CHUNK > SHARD:
            some = gath.at[pl.ds(0, chunks * CHUNK // SHARD)]
        else:
            some = gath.at[0, pl.ds(0, chunks * CHUNK)]
        pltpu.make_async_copy(some, some, xy_recv.at[b, sem]).wait()

    def first_own(b):
        for h in (0, 1):
            for d in (1, -1):
                xy_start(b, h, FIRST, place(h, 0, 0), place(h, d, 0), own=True)

    def second(b, q, own=False):
        for h in (0, 1):
            for d in (1, -1):
                xy_start(b, h, SECOND + q, place(h, SHIFT[q], 0), place(h, 0, d), own=own)

    def first_forward(b):
        xy_wait(b, FIRST, 4)
        for h in (0, 1):
            for d in (1, -1):
                xy_start(b, h, FIRST_FAR, place(h, -d, 0), place(h, d, 0), part=(1 - d) // 2)
        second(b, 1)
        second(b, 2)

    def first_far(b):
        xy_wait(b, FIRST_FAR, 2)
        second(b, 3)

    def second_forward(b, q):
        xy_wait(b, SECOND + q, 4)
        for h in (0, 1):
            for d in (1, -1):
                xy_start(b, h, SECOND_FAR, place(h, SHIFT[q], -d), place(h, 0, d), part=(1 - d) // 2)

    def second_far(b):
        xy_wait(b, SECOND_FAR, 8)

    SIGN = (1, -1)

    def tiles_wait(sem, count):
        some = amps.at[pl.ds(0, count)]
        pltpu.make_async_copy(some, some, sem).wait()

    def shard(owner_core, d):
        return amps.at[pl.ds(owner_core * (NZ * KT) + z_at(d) * KT, KT)]

    def z_start(dist, q):
        for way in (0, 1):
            part = shard(core, -SIGN[way] * (dist - 1)).at[q]
            if dist == FAR:
                part = part.at[pl.ds(way * (T // 2), T // 2)]
            remote(part, part, z_send, z_recv.at[dist - 1, q], z_dev(SIGN[way])).start()

    def to_sibling(dist):
        for way in (0,) if dist in (0, FAR) else (0, 1):
            part = shard(core, SIGN[way] * dist)
            remote(part, part, c_send, c_recv.at[0 if dist <= SOON else 1], sib_dev).start()

    def from_sibling(late):
        tiles_wait(c_recv.at[late], KT * (2 * (FAR - SOON) - 1 if late else 1 + 2 * SOON))

    def z_take(dist, q):
        tiles_wait(z_recv.at[dist - 1, q], 1 if dist == FAR else 2)
        if dist < FAR:
            z_start(dist + 1, q)
        if q == KT - 1:
            to_sibling(dist)

    def products(b, first, count):
        def body(n, carry):
            at = jnp.where(n < QUAD, quad_of(z, b, 0), quad_of(z, b, 1)) * QUAD + n % QUAD
            slot = n % 2 * (CORES * KT)
            for c in range(CORES):
                stage[pl.ds(slot + c * KT, KT)] = amps[pl.ds(c * (NZ * KT) + at * KT, KT)]
            for k in range(CAP):
                rows = pl.ds(pl.multiple_of(at * (2 * CAP * ROWS) + k * 2 * ROWS, 2 * ROWS), 2 * ROWS)
                group = gath[:, rows, :].astype(jnp.float32)
                for odd in (0, 1):
                    tile = group[:, odd * ROWS : (odd + 1) * ROWS, :].reshape(T, T).astype(jnp.bfloat16)
                    m = 2 * k + odd
                    which = inside(table[WHICH + m % CAP, at * CORES + m // CAP], KT)
                    prods[at * (2 * CAP) + m] = jnp.dot(
                        stage[slot + m // CAP * KT + which], tile, preferred_element_type=jnp.float32
                    )
            return carry

        lax.fori_loop(first, first + count, body, 0)

    def running(b):
        def body(t, acc):
            acc = jnp.where(table[KEEP, t] > 0, acc, 0.0) + prods[inside(table[PERM, t], TILES)]
            sums[t] = acc
            return acc

        lax.fori_loop(b * BATCH_TILES, (b + 1) * BATCH_TILES, body, jnp.zeros((T, T), jnp.float32))

    def slot_sum(b, r):
        at = b * RES + r
        return jnp.where(table[USED, at] > 0, sums[inside(table[LAST, at], TILES)], 0.0)

    def pick(b):
        def body(r, carry):
            value = slot_sum(b, r)
            own[r] = value if b == 0 else own[r] + value
            return carry

        lax.fori_loop(0, RES, body, 0)

    to_scalars = pltpu.make_async_copy(table_vmem, table, index_sem.at[0])

    def make_table():
        for c in index_copies:
            c.wait()
        place_table(table_vmem, cd, ab, owner, z, g)
        to_scalars.start()

    def table_done():
        to_scalars.wait()

    tiles_wait(amp_sem, KT)
    z_start(1, 0)
    first_own(0)
    second(0, 0, True)
    z_start(1, 1)
    z_start(1, 2)
    make_table()
    z_take(1, 0)
    first_own(1)
    z_take(1, 1)
    z_take(1, 2)
    first_forward(0)
    z_take(2, 0)
    z_take(2, 1)
    first_forward(1)
    z_take(2, 2)
    z_take(3, 0)
    z_take(3, 1)
    to_sibling(0)
    z_take(3, 2)
    first_far(0)
    z_take(4, 0)
    second_forward(0, 2)
    second_forward(0, 1)
    z_take(4, 1)
    z_take(4, 2)
    first_far(1)
    z_take(5, 0)
    z_take(5, 1)
    second(1, 0, True)
    z_take(5, 2)
    z_take(6, 0)
    second_forward(0, 0)
    second_forward(0, 3)
    z_take(6, 1)
    second_forward(1, 1)
    z_take(6, 2)
    second_forward(1, 0)
    from_sibling(0)
    z_take(7, 0)
    second_forward(1, 2)
    second_far(0)
    own_copy.wait()
    table_done()
    products(0, 6, 2)
    second_forward(1, 3)
    z_take(7, 1)
    z_take(7, 2)
    products(0, 4, 2)
    z_take(8, 0)
    products(0, 0, 2)
    products(0, 2, 2)
    second_far(1)
    z_take(8, 1)
    z_take(8, 2)
    running(0)
    pick(0)
    from_sibling(1)
    products(1, 0, 8)
    running(1)
    pick(1)

    def both(dist):
        return (dist,) if dist in (0, FAR) else (dist, -dist)

    def at_cross(d):
        return FAR + d if d != FAR else 0

    def blocks_wait(ref, sem, count):
        some = ref.at[pl.ds(0, count)]
        pltpu.make_async_copy(some, some, sem).wait()

    def cross_start(dist):
        for d in both(dist):
            remote(own.at[z_at(d) * CORES + sib], cross.at[at_cross(d)], x_send, x_recv.at[dist], sib_dev).start()

    def cross_wait(dist):
        blocks_wait(cross, x_recv.at[dist], len(both(dist)))

    hrows = T // PARTS

    def ring_start(way, dist, part):
        rows = pl.ds(part * hrows, hrows)
        hop = JUMP_SUM if dist == JUMP_SUM else 1
        remote(
            ring_out.at[2 * dist - 2 + way, rows], ring_in.at[2 * dist - 2 + way, rows],
            r_send, r_recv.at[dist - 1, part], z_dev(SIGN[way] * hop),
        ).start()

    def ring_wait(dist, part):
        some = ring_in.at[0, pl.ds(0, 2 * hrows if dist != FAR else hrows)]
        pltpu.make_async_copy(some, some, r_recv.at[dist - 1, part]).wait()

    def total(d, part):
        rows = pl.ds(part * hrows, hrows)
        return own[z_at(d) * CORES + core, rows, :] + cross[at_cross(d), rows, :]

    def arrived(way, dist, part):
        return ring_in[2 * dist - 2 + way, part * hrows : (part + 1) * hrows, :]

    def ring_step(dist, part):
        adds = dist != FAR and dist != JUMP_SUM - 1
        if adds:
            ring_wait(dist + 1, part)
        for way in (0, 1):
            if dist == FAR and part % 2 != way:
                continue
            value = total(FAR if dist == FAR else SIGN[way] * dist, part)
            if adds and (dist + 1 < FAR or part % 2 == way):
                value = value + arrived(way, dist + 1, part)
            ring_out[2 * dist - 2 + way, part * hrows : (part + 1) * hrows, :] = value
            ring_start(way, dist, part)

    def finish(part):
        value = total(0, part)
        for dist in sorted({1, JUMP_SUM}):
            ring_wait(dist, part)
            for way in (0, 1):
                value = value + arrived(way, dist, part)
        out_ref[part * hrows : (part + 1) * hrows, :] = value.astype(jnp.bfloat16)

    cross_start(8)
    cross_start(4)
    cross_wait(8)
    ring_step(8, 0)
    ring_step(8, 3)
    cross_wait(4)
    cross_start(7)
    ring_step(4, 0)
    ring_step(8, 2)
    ring_step(8, 1)
    ring_step(4, 1)
    cross_start(3)
    ring_step(4, 3)
    cross_start(6)
    cross_start(2)
    cross_start(5)
    ring_step(4, 2)
    cross_wait(7)
    cross_wait(3)
    ring_step(7, 0)
    cross_start(1)
    ring_step(3, 0)
    cross_wait(6)
    ring_step(7, 3)
    ring_step(3, 1)
    cross_wait(5)
    ring_step(7, 1)
    ring_step(3, 3)
    ring_step(7, 2)
    ring_step(3, 2)
    cross_wait(2)
    cross_start(0)
    ring_step(6, 0)
    ring_step(2, 0)
    ring_step(6, 3)
    ring_step(6, 1)
    ring_step(2, 3)
    ring_step(6, 2)
    ring_step(2, 1)
    cross_wait(0)
    ring_step(5, 0)
    ring_step(2, 2)
    ring_step(5, 3)
    ring_step(5, 1)
    ring_step(5, 2)
    cross_wait(1)
    ring_step(1, 2)
    ring_step(1, 3)
    ring_step(1, 0)
    ring_step(1, 1)
    finish(3)
    finish(0)
    finish(1)
    finish(2)

    some = gath.at[pl.ds(0, NP - 1)]
    pltpu.make_async_copy(some, some, xy_send).wait()
    tiles_wait(z_send, KT * (2 * FAR - 1))
    tiles_wait(c_send, KT * 2 * FAR)
    blocks_wait(own, x_send, NZ)
    blocks_wait(ring_out, r_send, 2 * FAR - 1)


def per_device(amplitudes, integrals, cd_index, ab_index, owner_map):
    shard = integrals.reshape(SHARD, T)
    dma = pltpu.SemaphoreType.DMA
    return pl.pallas_call(
        kernel,
        out_shape=jax.ShapeDtypeStruct((T, T), jnp.bfloat16),
        in_specs=[
            pl.BlockSpec(memory_space=pltpu.HBM),
            pl.BlockSpec(memory_space=pltpu.HBM),
            pl.BlockSpec(memory_space=pltpu.VMEM),
            pl.BlockSpec(memory_space=pltpu.HBM),
            pl.BlockSpec(memory_space=pltpu.HBM),
        ],
        out_specs=pl.BlockSpec(memory_space=pltpu.VMEM),
        scratch_shapes=[
            pltpu.SMEM((16, WIDE), jnp.int32),
            pltpu.VMEM((CAP, NI, NI), jnp.int32),
            pltpu.VMEM((CAP, NI, NI), jnp.int32),
            pltpu.VMEM((16, WIDE), jnp.int32),
            dma((2,)),
            pltpu.VMEM((NP, SHARD, T), jnp.bfloat16),
            pltpu.VMEM((CORES * NZ * KT, T, T), jnp.bfloat16),
            pltpu.VMEM((2 * CORES * KT, T, T), jnp.bfloat16),
            pltpu.VMEM((TILES, T, T), jnp.float32),
            pltpu.VMEM((TILES, T, T), jnp.float32),
            pltpu.VMEM((RES, T, T), jnp.float32),
            pltpu.VMEM((NZ, T, T), jnp.float32),
            pltpu.VMEM((2 * FAR, T, T), jnp.float32),
            pltpu.VMEM((2 * FAR, T, T), jnp.float32),
            dma, dma,
            dma, dma((BATCHES, 7)),
            dma, dma((FAR, KT)),
            dma, dma((2,)),
            dma, dma((FAR + 1,)),
            dma, dma((FAR, PARTS)),
        ],
        compiler_params=pltpu.CompilerParams(
            collective_id=0, has_side_effects=True, vmem_limit_bytes=VMEM
        ),
        name="ladder",
    )(cd_index.transpose(2, 0, 1), ab_index.transpose(2, 0, 1), owner_map.reshape(1, RES), amplitudes, shard)


def solution(mesh):
    return jax.shard_map(
        per_device,
        mesh=mesh,
        in_specs=(P("pair", "intg"), P("intg", None, None, "pair", None), P(), P(), P()),
        out_specs=P("pair", "intg"),
        check_vma=False,
    )
```

time: 383 us -> 74.4 us (0.19)
  waiting for transfers between devices: 260 us -> 0 us
  Pallas kernels: 0 us -> 72.8 us
  local copies, waits for them, and re-layouts: 59 us -> 1.38 us
  matrix products: 24.7 us -> 0 us
  other arithmetic: 23.6 us -> 0 us
  between operations: 13.2 us -> 0.01 us
    all_gather x2 -> x0, waiting for transfers between devices: 149 us -> none  [the longest x1 75.8 us: per_device(): columns = lax.all_gather(amplitudes, 'intg', axis=1, tiled=True)]
    reduce_scatter x1 -> x0, waiting for transfers between devices: 110 us -> none  [per_device(): lax.psum_scatter(partial_value, 'intg', scatter_dimension=0, tiled=True)]
    pallas_call x0 -> x1, Pallas kernels: none -> 72.8 us  [per_device(): pl.pallas_call(kernel, out_shape=jax.ShapeDtypeStruct((T, T), jnp.bfloat1...]
    gather x20 -> x0, local copies, waits for them, and re-layouts: 49.7 us -> none  [accumulate(): picked = jnp.take(blocks, cd_block, axis=1)]
    dot_general x20 -> x0, matrix products: 24.7 us -> none  [accumulate(): jnp.einsum('rgc,gcd->grd', picked, tile_block, preferred_element_type=jnp...]
    scatter-add x20 -> x0, other arithmetic: 20.7 us -> none  [accumulate(): return (partial_value.at[slot_block].add(products), None)]
    while x1 -> x0, local copies, waits for them, and re-layouts: 4.71 us -> none  [ladder(): lax.scan(accumulate, partial_value, (tiles_grouped, cd_grouped, slot_grou...]
  transfers between devices with their start and end apart: 3 -> 0, of which waited for: 3 -> 0; matrix products, arithmetic and copies ran while one was open for 2% -> 0% of each run, Pallas kernels for 0% -> 0%
where the time goes in v2:
time: 74.4 us; the launch traced here: 74.2 us
  Pallas kernels  72.8 us (98%)
  local copies, waits for them, and re-layouts  1.38 us (2%)
    pallas_call x1, Pallas kernels, per_device(): pl.pallas_call(kernel, out_shape=jax.ShapeDtypeStruct((T, T), jnp.bfloat1...  72.8 us

profile of v2, /device:TPU:6, one launch (start us, length us, event | category | flops | bytes accessed | tf_op | source)
XLA Modules:
  0.0 74.2 jit_solution(18061929117241446834)
XLA Ops:
  0.0 72.8 %ladder.1 = bf16[128,128]{1,0:T(8,128)(2,1)} custom-call(s32[5,32,32]{2,1,0:T(8,128)} %bitcast.5, s32[5,32,32]{2,1,0:T(8,128)} %bitcast.6, s32[1,32]{1,0:T(1,128)} %bitcast.7, bf16[128,384]{1,0:T(8,128)(2,1)} %amp_hbm.1, bf16[1280,128]{1,0:T(8,128)(2,1)} %bitcast.4), custom_call_target="tpu_custom_call" | custom-call | tf_op jit(solution)/shard_map/ladder/pallas_call | solution.py:465
  72.8 1.4 %copy.7 = bf16[128,128]{1,0:T(8,128)(2,1)} copy(bf16[128,128]{1,0:T(8,128)(2,1)} %ladder.1) | data formatting | bytes 65536

commit v3 on v2

--- a/solution.py
+++ b/solution.py
@@ -91,7 +91,7 @@
 def kernel(
     cd_hbm, ab_hbm, owner, amp_hbm, int_hbm, out_ref,
     table, cd, ab, table_vmem, index_sem,
-    gath, amps, stage, prods, sums, own, cross, ring_in, ring_out,
+    gath, amps, stage, prods, sums, own, cross, far_in, ring_in, ring_out,
     own_sem, amp_sem, xy_send, xy_recv, z_send, z_recv, c_send, c_recv,
     x_send, x_recv, r_send, r_recv,
 ):
@@ -177,8 +177,6 @@
         for h in (0, 1):
             for d in (1, -1):
                 xy_start(b, h, FIRST_FAR, place(h, -d, 0), place(h, d, 0), part=(1 - d) // 2)
-        second(b, 1)
-        second(b, 2)
 
     def first_far(b):
         xy_wait(b, FIRST_FAR, 2)
@@ -212,10 +210,10 @@
     def to_sibling(dist):
         for way in (0,) if dist in (0, FAR) else (0, 1):
             part = shard(core, SIGN[way] * dist)
-            remote(part, part, c_send, c_recv.at[0 if dist <= SOON else 1], sib_dev).start()
-
-    def from_sibling(late):
-        tiles_wait(c_recv.at[late], KT * (2 * (FAR - SOON) - 1 if late else 1 + 2 * SOON))
+            remote(part, part, c_send, c_recv.at[0 if dist <= SOON else 1 if dist < FAR else 2], sib_dev).start()
+
+    def from_sibling(n):
+        tiles_wait(c_recv.at[n], KT * (1 + 2 * SOON, 2 * (FAR - 1 - SOON), 1)[n])
 
     def z_take(dist, q):
         tiles_wait(z_recv.at[dist - 1, q], 1 if dist == FAR else 2)
@@ -275,73 +273,76 @@
     def table_done():
         to_scalars.wait()
 
+    first_own(1)
     tiles_wait(amp_sem, KT)
     z_start(1, 0)
     first_own(0)
+    z_start(1, 1)
+    make_table()
+    z_start(1, 2)
+    second(1, 0, True)
+    z_take(1, 0)
     second(0, 0, True)
-    z_start(1, 1)
-    z_start(1, 2)
-    make_table()
-    z_take(1, 0)
-    first_own(1)
     z_take(1, 1)
     z_take(1, 2)
     first_forward(0)
+    second(0, 1)
     z_take(2, 0)
+    first_forward(1)
     z_take(2, 1)
-    first_forward(1)
+    second(0, 2)
+    second(1, 1)
     z_take(2, 2)
     z_take(3, 0)
+    first_far(0)
     z_take(3, 1)
-    to_sibling(0)
     z_take(3, 2)
-    first_far(0)
+    second(1, 2)
     z_take(4, 0)
-    second_forward(0, 2)
-    second_forward(0, 1)
+    first_far(1)
     z_take(4, 1)
     z_take(4, 2)
-    first_far(1)
     z_take(5, 0)
+    second_forward(0, 1)
+    second_forward(0, 2)
     z_take(5, 1)
-    second(1, 0, True)
+    second_forward(0, 0)
     z_take(5, 2)
+    second_forward(0, 3)
+    to_sibling(0)
     z_take(6, 0)
-    second_forward(0, 0)
-    second_forward(0, 3)
+    second_forward(1, 3)
+    second_forward(1, 0)
+    from_sibling(0)
     z_take(6, 1)
+    second_forward(1, 2)
     second_forward(1, 1)
     z_take(6, 2)
-    second_forward(1, 0)
-    from_sibling(0)
-    z_take(7, 0)
-    second_forward(1, 2)
     second_far(0)
     own_copy.wait()
     table_done()
+    products(0, 0, 2)
+    z_take(7, 0)
+    products(0, 4, 2)
+    z_take(7, 1)
+    products(0, 2, 2)
+    z_take(7, 2)
     products(0, 6, 2)
-    second_forward(1, 3)
-    z_take(7, 1)
-    z_take(7, 2)
-    products(0, 4, 2)
+    running(0)
+    pick(0)
+    second_far(1)
     z_take(8, 0)
-    products(0, 0, 2)
-    products(0, 2, 2)
-    second_far(1)
+    from_sibling(1)
     z_take(8, 1)
     z_take(8, 2)
-    running(0)
-    pick(0)
-    from_sibling(1)
-    products(1, 0, 8)
+    products(1, 0, 4)
+    from_sibling(2)
+    products(1, 4, 4)
     running(1)
     pick(1)
 
     def both(dist):
-        return (dist,) if dist in (0, FAR) else (dist, -dist)
-
-    def at_cross(d):
-        return FAR + d if d != FAR else 0
+        return (0,) if dist == 0 else (dist, -dist)
 
     def blocks_wait(ref, sem, count):
         some = ref.at[pl.ds(0, count)]
@@ -349,7 +350,7 @@
 
     def cross_start(dist):
         for d in both(dist):
-            remote(own.at[z_at(d) * CORES + sib], cross.at[at_cross(d)], x_send, x_recv.at[dist], sib_dev).start()
+            remote(own.at[z_at(d) * CORES + sib], cross.at[FAR - 1 + d], x_send, x_recv.at[dist], sib_dev).start()
 
     def cross_wait(dist):
         blocks_wait(cross, x_recv.at[dist], len(both(dist)))
@@ -364,27 +365,41 @@
             r_send, r_recv.at[dist - 1, part], z_dev(SIGN[way] * hop),
         ).start()
 
+    def far_start(part):
+        way = part % 2
+        rows = pl.ds(part * hrows, hrows)
+        to = z_at(SIGN[way]) * CORES
+        block = z_at(FAR) * CORES
+        remote(
+            own.at[block + core, rows], ring_in.at[2 * FAR - 2 + way, rows],
+            r_send, r_recv.at[FAR - 1, part], (p, to + core),
+        ).start()
+        remote(
+            own.at[block + sib, rows], far_in.at[way, rows],
+            r_send, r_recv.at[FAR - 1, part], (p, to + sib),
+        ).start()
+
     def ring_wait(dist, part):
-        some = ring_in.at[0, pl.ds(0, 2 * hrows if dist != FAR else hrows)]
+        some = ring_in.at[0, pl.ds(0, 2 * hrows)]
         pltpu.make_async_copy(some, some, r_recv.at[dist - 1, part]).wait()
 
     def total(d, part):
         rows = pl.ds(part * hrows, hrows)
-        return own[z_at(d) * CORES + core, rows, :] + cross[at_cross(d), rows, :]
+        return own[z_at(d) * CORES + core, rows, :] + cross[FAR - 1 + d, rows, :]
 
     def arrived(way, dist, part):
         return ring_in[2 * dist - 2 + way, part * hrows : (part + 1) * hrows, :]
 
     def ring_step(dist, part):
-        adds = dist != FAR and dist != JUMP_SUM - 1
+        adds = dist != JUMP_SUM - 1
         if adds:
             ring_wait(dist + 1, part)
         for way in (0, 1):
-            if dist == FAR and part % 2 != way:
-                continue
-            value = total(FAR if dist == FAR else SIGN[way] * dist, part)
+            value = total(SIGN[way] * dist, part)
             if adds and (dist + 1 < FAR or part % 2 == way):
                 value = value + arrived(way, dist + 1, part)
+            if dist + 1 == FAR and part % 2 == way:
+                value = value + far_in[way, part * hrows : (part + 1) * hrows, :]
             ring_out[2 * dist - 2 + way, part * hrows : (part + 1) * hrows, :] = value
             ring_start(way, dist, part)
 
@@ -396,16 +411,14 @@
                 value = value + arrived(way, dist, part)
         out_ref[part * hrows : (part + 1) * hrows, :] = value.astype(jnp.bfloat16)
 
-    cross_start(8)
+    far_start(0)
+    far_start(1)
+    far_start(2)
+    far_start(3)
     cross_start(4)
-    cross_wait(8)
-    ring_step(8, 0)
-    ring_step(8, 3)
+    cross_start(7)
     cross_wait(4)
-    cross_start(7)
     ring_step(4, 0)
-    ring_step(8, 2)
-    ring_step(8, 1)
     ring_step(4, 1)
     cross_start(3)
     ring_step(4, 3)
@@ -455,8 +468,8 @@
     pltpu.make_async_copy(some, some, xy_send).wait()
     tiles_wait(z_send, KT * (2 * FAR - 1))
     tiles_wait(c_send, KT * 2 * FAR)
-    blocks_wait(own, x_send, NZ)
-    blocks_wait(ring_out, r_send, 2 * FAR - 1)
+    blocks_wait(own, x_send, NZ - 1)
+    blocks_wait(ring_out, r_send, 2 * FAR)
 
 
 def per_device(amplitudes, integrals, cd_index, ab_index, owner_map):
@@ -485,14 +498,15 @@
             pltpu.VMEM((TILES, T, T), jnp.float32),
             pltpu.VMEM((TILES, T, T), jnp.float32),
             pltpu.VMEM((RES, T, T), jnp.float32),
-            pltpu.VMEM((NZ, T, T), jnp.float32),
+            pltpu.VMEM((NZ - 1, T, T), jnp.float32),
+            pltpu.VMEM((2, T, T), jnp.float32),
             pltpu.VMEM((2 * FAR, T, T), jnp.float32),
             pltpu.VMEM((2 * FAR, T, T), jnp.float32),
             dma, dma,
             dma, dma((BATCHES, 7)),
             dma, dma((FAR, KT)),
-            dma, dma((2,)),
-            dma, dma((FAR + 1,)),
+            dma, dma((3,)),
+            dma, dma((FAR,)),
             dma, dma((FAR, PARTS)),
         ],
         compiler_params=pltpu.CompilerParams(

time: 74.4 us -> 73 us (0.981)
  Pallas kernels: 72.8 us -> 71 us
    pallas_call x1, Pallas kernels: 72.8 us -> 71 us  [per_device(): pl.pallas_call(kernel, out_shape=jax.ShapeDtypeStruct((T, T), jnp.bfloat1...]
where the time goes in v3:
time: 73 us; the launch traced here: 72.4 us
  Pallas kernels  71 us (97%)
  local copies, waits for them, and re-layouts  1.38 us (2%)
    pallas_call x1, Pallas kernels, per_device(): pl.pallas_call(kernel, out_shape=jax.ShapeDtypeStruct((T, T), jnp.bfloat1...  71 us

profile of v3, /device:TPU:6, one launch (start us, length us, event | category | flops | bytes accessed | tf_op | source)
XLA Modules:
  0.0 72.4 jit_solution(5933815667791972852)
XLA Ops:
  0.0 71.0 %ladder.1 = bf16[128,128]{1,0:T(8,128)(2,1)} custom-call(s32[5,32,32]{2,1,0:T(8,128)} %bitcast.5, s32[5,32,32]{2,1,0:T(8,128)} %bitcast.6, s32[1,32]{1,0:T(1,128)} %bitcast.7, bf16[128,384]{1,0:T(8,128)(2,1)} %amp_hbm.1, bf16[1280,128]{1,0:T(8,128)(2,1)} %bitcast.4), custom_call_target="tpu_custom_call" | custom-call | tf_op jit(solution)/shard_map/ladder/pallas_call | solution.py:478
  71.0 1.4 %copy.7 = bf16[128,128]{1,0:T(8,128)(2,1)} copy(bf16[128,128]{1,0:T(8,128)(2,1)} %ladder.1) | data formatting | bytes 65536

commit v4 on v3

--- a/solution.py
+++ b/solution.py
@@ -240,7 +240,7 @@
                     )
             return carry
 
-        lax.fori_loop(first, first + count, body, 0)
+        lax.fori_loop(first, first + count, body, 0, unroll=2)
 
     def running(b):
         def body(t, acc):
@@ -248,7 +248,7 @@
             sums[t] = acc
             return acc
 
-        lax.fori_loop(b * BATCH_TILES, (b + 1) * BATCH_TILES, body, jnp.zeros((T, T), jnp.float32))
+        lax.fori_loop(b * BATCH_TILES, (b + 1) * BATCH_TILES, body, jnp.zeros((T, T), jnp.float32), unroll=8)
 
     def slot_sum(b, r):
         at = b * RES + r
@@ -260,7 +260,7 @@
             own[r] = value if b == 0 else own[r] + value
             return carry
 
-        lax.fori_loop(0, RES, body, 0)
+        lax.fori_loop(0, RES, body, 0, unroll=8)
 
     to_scalars = pltpu.make_async_copy(table_vmem, table, index_sem.at[0])
 

time: 73 us -> 71.2 us (0.975)
  Pallas kernels: 71 us -> 69.5 us
    pallas_call x1, Pallas kernels: 71 us -> 69.5 us  [per_device(): pl.pallas_call(kernel, out_shape=jax.ShapeDtypeStruct((T, T), jnp.bfloat1...]
where the time goes in v4:
time: 71.2 us; the launch traced here: 70.8 us
  Pallas kernels  69.5 us (98%)
  local copies, waits for them, and re-layouts  1.38 us (2%)
    pallas_call x1, Pallas kernels, per_device(): pl.pallas_call(kernel, out_shape=jax.ShapeDtypeStruct((T, T), jnp.bfloat1...  69.5 us

profile of v4, /device:TPU:6, one launch (start us, length us, event | category | flops | bytes accessed | tf_op | source)
XLA Modules:
  0.0 70.8 jit_solution(3378340351498866604)
XLA Ops:
  0.0 69.5 %ladder.1 = bf16[128,128]{1,0:T(8,128)(2,1)} custom-call(s32[5,32,32]{2,1,0:T(8,128)} %bitcast.5, s32[5,32,32]{2,1,0:T(8,128)} %bitcast.6, s32[1,32]{1,0:T(1,128)} %bitcast.7, bf16[128,384]{1,0:T(8,128)(2,1)} %amp_hbm.1, bf16[1280,128]{1,0:T(8,128)(2,1)} %bitcast.4), custom_call_target="tpu_custom_call" | custom-call | tf_op jit(solution)/shard_map/ladder/pallas_call | solution.py:478
  69.5 1.4 %copy.7 = bf16[128,128]{1,0:T(8,128)(2,1)} copy(bf16[128,128]{1,0:T(8,128)(2,1)} %ladder.1) | data formatting | bytes 65536

commit v5 on v4

--- a/solution.py
+++ b/solution.py
@@ -240,7 +240,7 @@
                     )
             return carry
 
-        lax.fori_loop(first, first + count, body, 0, unroll=2)
+        lax.fori_loop(first, first + count, body, 0, unroll=count)
 
     def running(b):
         def body(t, acc):

time: 71.2 us -> 71.2 us (level)
  no operation moved by 1% of the time
where the time goes in v5:
time: 71.2 us; the launch traced here: 70.5 us
  Pallas kernels  69.1 us (97%)
  local copies, waits for them, and re-layouts  1.38 us (2%)
    pallas_call x1, Pallas kernels, per_device(): pl.pallas_call(kernel, out_shape=jax.ShapeDtypeStruct((T, T), jnp.bfloat1...  69.1 us

profile of v5, /device:TPU:6, one launch (start us, length us, event | category | flops | bytes accessed | tf_op | source)
XLA Modules:
  0.0 70.5 jit_solution(512451906069415044)
XLA Ops:
  0.0 69.1 %ladder.1 = bf16[128,128]{1,0:T(8,128)(2,1)} custom-call(s32[5,32,32]{2,1,0:T(8,128)} %bitcast.5, s32[5,32,32]{2,1,0:T(8,128)} %bitcast.6, s32[1,32]{1,0:T(1,128)} %bitcast.7, bf16[128,384]{1,0:T(8,128)(2,1)} %amp_hbm.1, bf16[1280,128]{1,0:T(8,128)(2,1)} %bitcast.4), custom_call_target="tpu_custom_call" | custom-call | tf_op jit(solution)/shard_map/ladder/pallas_call | solution.py:478
  69.1 1.4 %copy.7 = bf16[128,128]{1,0:T(8,128)(2,1)} copy(bf16[128,128]{1,0:T(8,128)(2,1)} %ladder.1) | data formatting | bytes 65536
